TPU v7x, 32 devices: a whole 2x2x4 slice. The times are simulated.
32 devices in a mesh: grp: 2 (over y), dev: 8 (over z, core), pool: 2 (over x).
Axes of the slice: x: 2, y: 2, z: 4, core: 2. Of those that a mesh axis runs over, the one named last changes fastest.
Arguments:
- hidden_in: bfloat16 [32, 2880], P(('grp', 'pool'), 'dev'), parts along dimension 0, may hold values from -4 to 4
- queries: bfloat16 [32, 8, 512], P(('grp', 'dev'), 'pool'), parts along dimension 0, may hold values from -40 to 40
- new_keyval: bfloat16 [32, 8, 128], P(('grp', 'dev'), 'pool'), parts along dimension 0, may hold values from -4 to 4
- cache_entries: bfloat16 [320, 2048, 128], P(('grp', 'dev', 'pool')), parts along dimension 0, may hold values from -4 to 4
- slot_table: int32 [32, 8], P('grp'), parts along dimension 0, may hold values from 0 to 159, as said below
- context_len: int32 [32], P('grp'), parts along dimension 0, may hold values from 1 to 2048, 16384 in all
- out_proj: bfloat16 [4096, 2880], P('pool', 'dev'), may hold values from -0.09375 to 0.09375
- norm_gain: float32 [2880], replicated, may hold values from 0.5 to 1.5
- expert_ids: int32 [32, 4], P('grp'), parts along dimension 0, may hold values from 0 to 7, all different within a row; in each aligned block of 16 rows (0 to 15, 16 to 31, ...) at most 16 rows name the same one
- expert_gates: float32 [32, 4], P('grp'), parts along dimension 0, may hold values from 0.05 to 0.5
- expert_in: bfloat16 [8, 2880, 2, 2880], P('dev', None, None, 'pool'), may hold values from -0.109375 to 0.109375
- expert_down: bfloat16 [8, 2880, 2880], P('dev', 'pool'), may hold values from -0.109375 to 0.109375
Outputs:
- hidden_out: bfloat16 [32, 2880], P(('grp', 'pool'), 'dev'), parts along dimension 0
There are 2 independent parts, one for each index of `grp`. A program takes and returns all parts, laid end to end along the dimension named above; an argument that names none is the same for every part. Nothing has to cross between parts.
Inputs may be any that keep to these rules, and one draw needn't show every extreme that they name: `slot_table`: no two request-heads share a slot. The slot of request r and kv head h lies on the device of flat index slot // 10, counted with dev major and pool minor, and the pool index of that device is h // 4. `expert_ids`: each request names 4 different experts; no expert is named by more than 16 requests.
All inputs are finite; a program needn't handle non-finite values.
Results may differ from a plain program's by a relative error of at most 0.012.
Values may be sent and summed in bfloat16 or wider, within the bound.
A program may use at most 128 MiB of HBM per device.

v0:
```python
import math

import jax
import jax.numpy as jnp
from jax import lax
from jax.sharding import PartitionSpec as P


def attend(query_slot, newkv_slot, cache_entries, slot_length):
    slot_count, context, pair_width = cache_entries.shape
    head_dim = pair_width // 2
    group_heads = query_slot.shape[1] // head_dim
    inv_root = 1.0 / math.sqrt(head_dim)
    query_heads = query_slot.reshape(slot_count, group_heads, head_dim)
    scores = (
        jnp.einsum(
            "sgd,scd->sgc",
            query_heads,
            cache_entries[:, :, :head_dim],
            preferred_element_type=jnp.float32,
        )
        * inv_root
    )
    in_range = jnp.arange(context, dtype=jnp.int32)[None, :] < slot_length[:, None]
    scores = jnp.where(in_range[:, None, :], scores, -1e30)
    own_score = (
        jnp.einsum(
            "sgd,sd->sg", query_heads, newkv_slot[:, :head_dim], preferred_element_type=jnp.float32
        )
        * inv_root
    )
    highest = jnp.maximum(jnp.max(scores, axis=2), own_score)
    raised = jnp.exp(scores - highest[:, :, None])
    own_raised = jnp.exp(own_score - highest)
    denominator = jnp.sum(raised, axis=2) + own_raised
    probs_cache = (raised / denominator[:, :, None]).astype(jnp.bfloat16)
    probs_own = (own_raised / denominator).astype(jnp.bfloat16)
    mixed_out = jnp.einsum(
        "sgc,scd->sgd",
        probs_cache,
        cache_entries[:, :, head_dim:],
        preferred_element_type=jnp.float32,
    )
    mixed_out = mixed_out + probs_own.astype(jnp.float32)[:, :, None] * newkv_slot[
        :, None, head_dim:
    ].astype(jnp.float32)
    return mixed_out.astype(jnp.bfloat16).reshape(slot_count, group_heads * head_dim)


def expert_apply(inputs, expert_in, expert_down):
    hidden_units = expert_down.shape[1]
    both_parts = jnp.dot(
        inputs,
        expert_in.reshape(expert_in.shape[1], 2 * hidden_units),
        preferred_element_type=jnp.float32,
    )
    gate_part = both_parts[:, :hidden_units]
    up_part = both_parts[:, hidden_units:]
    activated = (gate_part * jax.nn.sigmoid(1.702 * gate_part) * (up_part + 1.0)).astype(
        jnp.bfloat16
    )
    return jnp.dot(activated, expert_down[0], preferred_element_type=jnp.float32)


def body(
    hidden_in,
    queries,
    new_keyval,
    cache_entries,
    slot_table,
    context_len,
    out_proj,
    norm_gain,
    expert_ids,
    expert_gates,
    expert_in,
    expert_down,
):
    dev_count = lax.axis_size("dev")
    pool_count = lax.axis_size("pool")
    dev_index = lax.axis_index("dev")
    pool_index = lax.axis_index("pool")
    slot_count = cache_entries.shape[0]
    requests = slot_table.shape[0]
    pool_heads = queries.shape[1]
    query_width = queries.shape[2]
    pair_width = new_keyval.shape[2]
    query_all, keyval_all = (
        lax.all_gather(queries, "dev", axis=0, tiled=True),
        lax.all_gather(new_keyval, "dev", axis=0, tiled=True),
    )
    query_rows = query_all.reshape(requests * pool_heads, query_width)
    keyval_rows = keyval_all.reshape(requests * pool_heads, pair_width)
    pool_slots = lax.dynamic_slice_in_dim(
        slot_table, pool_index * pool_heads, pool_heads, 1
    ).reshape(-1)
    first_slot = (dev_index * pool_count + pool_index) * slot_count
    own_ids = first_slot + jnp.arange(slot_count, dtype=jnp.int32)
    owner_mask = pool_slots[None, :] == own_ids[:, None]
    owner_pick = owner_mask.astype(jnp.bfloat16)
    query_slot = jnp.dot(owner_pick, query_rows, preferred_element_type=jnp.float32).astype(
        jnp.bfloat16
    )
    newkv_slot = jnp.dot(owner_pick, keyval_rows, preferred_element_type=jnp.float32).astype(
        jnp.bfloat16
    )
    length_rows = jnp.repeat(context_len, pool_heads)
    slot_length = jnp.sum(jnp.where(owner_mask, length_rows[None, :], 0), axis=1)
    attn_slot = attend(query_slot, newkv_slot, cache_entries, slot_length)
    all_outputs = lax.all_gather(attn_slot, "dev", axis=0, tiled=True)
    column_ids = (
        (jnp.arange(dev_count, dtype=jnp.int32)[:, None] * pool_count + pool_index) * slot_count
        + jnp.arange(slot_count, dtype=jnp.int32)[None, :]
    ).reshape(-1)
    column_pick = (pool_slots[:, None] == column_ids[None, :]).astype(jnp.bfloat16)
    attn_rows = jnp.dot(column_pick, all_outputs, preferred_element_type=jnp.float32).astype(
        jnp.bfloat16
    )
    attn_group = attn_rows.reshape(requests, pool_heads * query_width)
    projected = lax.psum_scatter(
        jnp.dot(attn_group, out_proj, preferred_element_type=jnp.float32),
        "pool",
        scatter_dimension=0,
        tiled=True,
    )
    residual = (hidden_in.astype(jnp.float32) + projected).astype(jnp.bfloat16)
    row_block, col_block = hidden_in.shape
    blocks = lax.all_gather(residual[None], ("dev", "pool"), axis=0, tiled=True)
    full_rows = (
        blocks.reshape(dev_count, pool_count, row_block, col_block)
        .transpose(1, 2, 0, 3)
        .reshape(requests, dev_count * col_block)
    )
    widened = full_rows.astype(jnp.float32)
    normed = (
        widened * lax.rsqrt(jnp.mean(widened * widened, axis=1, keepdims=True) + 1e-05) * norm_gain
    ).astype(jnp.bfloat16)
    expert_hit = expert_ids == dev_index
    route_weight = jnp.sum(jnp.where(expert_hit, expert_gates, 0.0), axis=1)
    routed = jnp.any(expert_hit, axis=1)
    top_count = expert_ids.shape[1]
    capacity = min(requests, 2 * requests * top_count // dev_count)
    position = jnp.cumsum(routed.astype(jnp.int32)) - 1
    selector = (position[None, :] == jnp.arange(capacity, dtype=jnp.int32)[:, None]) & routed[
        None, :
    ]
    chosen = jnp.dot(
        selector.astype(jnp.bfloat16), normed, preferred_element_type=jnp.float32
    ).astype(jnp.bfloat16)
    computed = expert_apply(chosen, expert_in, expert_down)
    back_rows = computed[jnp.clip(position, 0, capacity - 1)]
    expert_terms = jnp.where(routed[:, None], back_rows, 0.0) * route_weight[:, None]
    arranged = (
        expert_terms.reshape(pool_count, row_block, dev_count, col_block)
        .transpose(2, 0, 1, 3)
        .reshape(dev_count * pool_count, row_block, col_block)
    )
    mixture = lax.psum_scatter(arranged, ("dev", "pool"), scatter_dimension=0, tiled=True)[0]
    return (residual.astype(jnp.float32) + mixture).astype(jnp.bfloat16)


def solution(mesh):
    return jax.shard_map(
        body,
        mesh=mesh,
        in_specs=(
            P(("grp", "pool"), "dev"),
            P(("grp", "dev"), "pool", None),
            P(("grp", "dev"), "pool", None),
            P(("grp", "dev", "pool"), None, None),
            P("grp", None),
            P("grp"),
            P("pool", "dev"),
            P(),
            P("grp", None),
            P("grp", None),
            P("dev", None, None, "pool"),
            P("dev", "pool", None),
        ),
        out_specs=P(("grp", "pool"), "dev"),
        check_vma=False,
    )
```

profile of v0, /device:TPU:0, one launch (start us, length us, event | category | flops | bytes accessed | tf_op | source)
XLA Modules:
  0.0 175.3 jit_solution(17315184461865475452)
XLA Ops:
  6.5 0.8 select_reduce_fusion
  7.5 0.7 constant_dynamic-slice_fusion
  8.4 15.9 %all_gather.12 = bf16[16,4,512]{2,1,0:T(4,128)(2,1)S(1)} all-gather(bf16[2,4,512]{2,1,0:T(4,128)(2,1)} %param.13), channel_id=1, replica_groups=mesh['grp'=2,'dev'=8,'pool'=2] {'dev'}, dimensions={0}, use_global_device_ids=true | all-gather | bytes 73728 | tf_op jit(solution)/shard_map/all_gather | solution.py:89
  24.3 0.2 convolution_convert_fusion.2
  24.4 0.1 reshape.152
  24.5 0.7 broadcast_in_dim.68
  25.4 0.2 fusion.38
  25.6 0.1 iota_compare_fusion
  25.7 13.0 %all_gather.13 = bf16[16,4,128]{2,1,0:T(4,128)(2,1)S(1)} all-gather(bf16[2,4,128]{2,1,0:T(4,128)(2,1)} %param.14), channel_id=1, replica_groups=mesh['grp'=2,'dev'=8,'pool'=2] {'dev'}, dimensions={0}, use_global_device_ids=true | all-gather | bytes 18432 | tf_op jit(solution)/shard_map/all_gather | solution.py:90
  38.6 0.2 convolution_convert_fusion.3
  38.9 0.1 fusion.46
  39.0 4.0 %fusion.60 = (f32[10,8]{1,0:T(8,128)S(1)}, f32[10,8,2048]{2,1,0:T(8,128)S(1)}) fusion(bf16[10,8,64]{2,1,0:T(8,128)(2,1)S(1)} %reshape.152, bf16[10,2048,128]{2,1,0:T(8,128)(2,1)} %param.15, pred[10,2048]{1,0:T(8,128)(4,1)S(1)} %iota_compare_fusion), kind=kOutput, calls=%fused_computation.77 | convolution fusion | flops 21462960 | bytes 5929280 | tf_op jit(solution)/shard_map/sgd,scd->sgc/dot_general | solution.py:16
  43.1 0.3 fusion.19
  43.4 1.6 fusion.16
  45.0 0.1 reshape.176
  45.1 14.0 %all-gather.1 = bf16[8,10,512]{2,1,0:T(8,128)(2,1)S(1)} all-gather(bf16[1,10,512]{2,1,0:T(8,128)(2,1)S(1)} %reshape.176), channel_id=1, replica_groups=mesh['grp'=2,'dev'=8,'pool'=2] {'dev'}, dimensions={0}, use_global_device_ids=true | all-gather | bytes 92160 | tf_op jit(solution)/shard_map/all_gather | solution.py:110
  59.2 0.2 convolution_convert_fusion.1
  59.5 0.5 fusion.61
  60.0 8.3 %all-reduce = f32[16,360]{1,0:T(8,128)S(1)} all-reduce(f32[16,360]{1,0:T(8,128)S(1)} %fusion.61), channel_id=3, replica_groups=mesh['grp'=2,'dev'=8,'pool'=2] {'pool'}, use_global_device_ids=true, to_apply=%region_3.4.clone | all-reduce | flops 5760 | bytes 46080
  68.3 0.6 dynamic-slice
  69.6 29.5 %all-gather = bf16[128,360]{1,0:T(8,128)(2,1)S(1)} all-gather(bf16[8,360]{1,0:T(8,128)(2,1)S(1)} %fusion.36), channel_id=2, replica_groups=mesh['grp'=2,'dev'=8,'pool'=2] {'dev','pool'}, dimensions={0}, use_global_device_ids=true | all-gather | bytes 97920 | tf_op jit(solution)/shard_map/all_gather | solution.py:128
  99.1 0.1 multiply_reduce_fusion
  99.2 0.1 reshape.159
  99.6 0.1 fusion.39
  99.8 8.8 %fusion.12 = f32[16,2880]{1,0:T(8,128)S(1)} fusion(bf16[2880,2880]{0,1:T(8,128)(2,1)} %bitcast.51, f32[16,2880]{1,0:T(8,128)S(1)} %reshape.159, f32[2880]{0:T(1024)S(1)} %copy-done.2, f32[16]{0:T(128)S(1)} %rsqrt.12, s32[16]{0:T(128)S(1)} %get-tuple-element.6, pred[16]{0:T(512)(128)(4,1)S(1)} %reduce_or.9), kind=kOutput, calls=%fused_computation.11 | convolution fusion | flops 267080192 | bytes 16969104 | tf_op jit(solution)/shard_map/dot_general | solution.py:52
  108.6 4.7 %fusion = f32[16,2880]{1,0:T(8,128)S(1)} fusion(bf16[1,1440,2880]{2,1,0:T(8,128)(2,1)} %param.23, f32[16,2880]{1,0:T(8,128)S(1)} %fusion.12), kind=kOutput, calls=%fused_computation.1 | convolution fusion | flops 132894720 | bytes 8675328 | tf_op jit(solution)/shard_map/dot_general | solution.py:62
  113.3 0.6 gather_fusion
  113.9 0.2 gather.6
  114.1 0.1 multiply_bitcast_fusion
  114.2 0.7 copy.35
  115.0 52.2 %reduce-scatter.4.cloned.1.call-done = f32[1,8,360]{2,1,0:T(8,128)} async-done(((f32[16,8,360]{2,1,0:T(8,128)}), f32[1,8,360]{2,1,0:T(8,128)}) %reduce-scatter.4.cloned.1.call-update) | async-done | bytes 11536
  167.2 1.3 fusion.37
  (38 shorter events, 1.2 us)
Async XLA Ops:
  6.5 53.0 %copy-start = (bf16[2048,360]{0,1:T(8,128)(2,1)S(1)}, bf16[2048,360]{0,1:T(8,128)(2,1)}, u32[]{:S(2)}) copy-start(bf16[2048,360]{0,1:T(8,128)(2,1)} %param.18) | copy-start | bytes 4423684
  6.5 160.6 %reduce-scatter.4.cloned.1.call-start = ((), (), s32[]{:S(2)}) async-start(), calls=%async_computation.1 | async-start | bytes 208896
  25.4 18.0 %copy-start.1 = (bf16[10,2048,128]{2,1,0:T(8,128)(2,1)S(1)}, bf16[10,2048,128]{2,1,0:T(8,128)(2,1)}, u32[]{:S(2)}) copy-start(bf16[10,2048,128]{2,1,0:T(8,128)(2,1)} %param.15) | copy-start | bytes 15728644
  43.3 25.0 %copy-start.4 = (u32[32]{0:T(128)S(1)}, u32[32]{0:T(128)}, u32[]{:S(2)}) copy-start(u32[32]{0:T(128)} %constant.58) | copy-start | bytes 388
  43.3 26.2 %copy-start.3 = (bf16[8,360]{1,0:T(8,128)(2,1)S(1)}, bf16[8,360]{1,0:T(8,128)(2,1)}, u32[]{:S(2)}) copy-start(bf16[8,360]{1,0:T(8,128)(2,1)} %param.12) | copy-start | bytes 17284
  43.4 56.4 %copy-start.2 = (f32[2880]{0:T(1024)S(1)}, f32[2880]{0:T(1024)}, u32[]{:S(2)}) copy-start(f32[2880]{0:T(1024)} %param.19) | copy-start | bytes 34564
Sparse Core Ops, SparseCore 0:
  115.1 52.0 reduce-scatter.3
where the time goes:
time: 176 us; the launch traced here: 175 us
  blocking collectives  80.6 us (46%)
  waiting for transfers between devices  52.2 us (30%)
  matrix products  20.3 us (12%)
  between operations  14.2 us (8%)
  local copies, waits for them, and re-layouts  4.71 us (3%)
  other arithmetic  3.28 us (2%)
    unnamed x2, waiting for transfers between devices  52.2 us
    all_gather x1, blocking collectives, body(): blocks = lax.all_gather(residual[None], ('dev', 'pool'), axis=0, tiled=True)  29.5 us
    all_gather x1, blocking collectives, body(): lax.all_gather(queries, 'dev', axis=0, tiled=True)  15.9 us
    all_gather x1, blocking collectives, body(): all_outputs = lax.all_gather(attn_slot, 'dev', axis=0, tiled=True)  14 us
    all_gather x1, blocking collectives, body(): lax.all_gather(new_keyval, 'dev', axis=0, tiled=True)  13 us
    dot_general x1, matrix products, expert_apply(): jnp.dot(inputs, expert_in.reshape(expert_in.shape[1], 2 * hidden_units),...  8.76 us
    unnamed x1, blocking collectives  8.31 us
    dot_general x1, matrix products, expert_apply(): jnp.dot(activated, expert_down[0], preferred_element_type=jnp.float32)  4.7 us
  transfers between devices with their start and end apart: 1, of which 1 were waited for; matrix products, arithmetic and copies ran while one was open for 0% of the time, Pallas kernels for 0%

commit v1 on v0

v1 whole, which is shorter than its diff:
```python
import functools
import math

import jax
import jax.numpy as jnp
from jax import lax
from jax.experimental import pallas as pl
from jax.experimental.pallas import tpu as pltpu
from jax.sharding import PartitionSpec as P

F32, BF16 = jnp.float32, jnp.bfloat16
NT = (((1,), (1,)), ((), ()))


def up_to(value, step):
    return -(-value // step) * step


def div(x, n):
    if n & (n - 1) == 0:
        return lax.shift_right_logical(x, jnp.full_like(x, n.bit_length() - 1))
    return lax.div(x, jnp.full_like(x, n))


def mod(x, n):
    if n & (n - 1) == 0:
        return x & (n - 1)
    return lax.rem(x, jnp.full_like(x, n))


def iota(shape, dim):
    return lax.broadcasted_iota(jnp.int32, shape, dim)


def pieces(rows):
    for count in (6, 5, 4, 3, 2):
        if rows % count == 0 and (rows // count) % 16 == 0:
            return count
    return 1


def dot(a, b):
    return jnp.dot(a, b, preferred_element_type=F32)


def dot_nt(a, b):
    return lax.dot_general(a, b, NT, preferred_element_type=F32)


def kernel(
    devs,
    pools,
    pool_heads,
    slots,
    col_block,
    hidden,
    pack,
    table_t,
    lengths,
    gain,
    ids_t,
    gates_t,
    cache_hbm,
    proj_hbm,
    in_hbm,
    down_hbm,
    out,
    cache,
    proj_w,
    in_w,
    down_w,
    g_query,
    g_attn,
    g_sum,
    g_resid,
    s_moe,
    g_moe,
    g_last,
    acc,
    cache_sem,
    proj_sem,
    in_sem,
    down_sem,
    dev_send,
    dev_recv,
    pool_send,
    pool_recv,
):
    me_d, me_p = lax.axis_index("dev"), lax.axis_index("pool")
    requests = table_t.shape[1]
    row_block = hidden.shape[0]
    head_dim = cache.shape[2] // 2
    pair = 2 * head_dim
    width = proj_w.shape[1] // pool_heads
    group = width // head_dim
    half_w = width // 2
    half_g = group // 2
    pack_rows = pack.shape[0]
    part = pack_rows // 2
    per_dev = requests // devs
    chunks = in_w.shape[1]
    inv_root = 1.0 / math.sqrt(head_dim)

    cache_copies = [
        pltpu.make_async_copy(cache_hbm.at[s], cache.at[s], cache_sem.at[s]) for s in range(slots)
    ]
    for copy in cache_copies:
        copy.start()
    proj_copy = pltpu.make_async_copy(proj_hbm, proj_w, proj_sem.at[0])
    proj_copy.start()

    def in_copy(part_at, c):
        return pltpu.make_async_copy(
            in_hbm.at[part_at, c], in_w.at[part_at, c], in_sem.at[part_at, c]
        )

    def down_copy(c):
        return pltpu.make_async_copy(down_hbm.at[c], down_w.at[c], down_sem.at[c])

    for c in range(chunks):
        in_copy(0, c).start()
        in_copy(1, c).start()
        down_copy(c).start()

    barrier = pltpu.get_barrier_semaphore()
    for axis, me, n in (("dev", me_d, devs), ("pool", me_p, pools)):
        for k in range(1, n):
            pl.semaphore_signal(
                barrier,
                inc=1,
                device_id={axis: lax.rem(me + k, n)},
                device_id_type=pl.DeviceIdType.MESH,
            )
    pl.semaphore_wait(barrier, devs + pools - 2)

    def exchange(axis, me, n, phase, dst, source=None):
        send, recv = (dev_send, dev_recv) if axis == "dev" else (pool_send, pool_recv)
        copies = []
        for k in range(1, n):
            peer = lax.rem(me + k, n)
            copies.append(
                pltpu.make_async_remote_copy(
                    src_ref=dst.at[me] if source is None else source.at[peer],
                    dst_ref=dst.at[me],
                    send_sem=send.at[phase, k - 1],
                    recv_sem=recv.at[phase, k - 1],
                    device_id={axis: peer},
                    device_id_type=pl.DeviceIdType.MESH,
                )
            )
            copies[-1].start()
        return copies

    def finish(copies):
        for copy in copies:
            copy.wait()

    g_query[me_d] = pack[...]
    sent = exchange("dev", me_d, devs, 0, g_query)

    table = table_t[...].astype(F32)
    rows = slots * group
    first = ((me_d * pools + me_p) * slots).astype(F32)
    row_id = div(iota((rows, 1), 0), group).astype(F32) + first
    len_row = lengths[...].astype(F32)
    cols = devs * pack_rows
    req_at, col_at = iota((requests, cols), 0), iota((requests, cols), 1)
    inner = mod(col_at, part)
    same_request = div(col_at, pack_rows) * per_dev + div(inner, pool_heads) == req_at
    length = jnp.zeros((rows, 1), F32)
    pick = jnp.zeros((rows, cols), F32)
    own_rows = []
    for h in range(pool_heads):
        line = jnp.zeros((1, requests), F32)
        for p in range(pools):
            at = p * pool_heads + h
            line = line + jnp.where(me_p == p, table[at : at + 1, :], 0.0)
        own_rows.append(line)
        mine = jnp.where(line == row_id, 1.0, 0.0)
        length = length + jnp.sum(mine * len_row, axis=1, keepdims=True)
        place = jnp.where(same_request & (mod(inner, pool_heads) == h), 1.0, 0.0)
        pick = pick + dot(mine.astype(BF16), place.astype(BF16))
    row_at, col_at = iota((rows, cols), 0), iota((rows, cols), 1)
    right_half = div(mod(col_at, pack_rows), part) == div(mod(row_at, group), half_g)
    pick = jnp.where(right_half, pick, 0.0).astype(BF16)
    own_g = div(iota((rows, half_w), 1), head_dim) == mod(iota((rows, half_w), 0), half_g)
    fold_at, fold_to = iota((half_w, pair), 0), iota((half_w, pair), 1)
    fold = jnp.where(mod(fold_at, head_dim) == fold_to, 1.0, 0.0).astype(BF16)
    diagonal = iota((requests, requests), 0) == iota((requests, requests), 1)

    def column(line):
        return jnp.sum(jnp.where(diagonal, line, 0.0), axis=1, keepdims=True)

    slot_rows = g_attn.shape[1]
    lane = iota((1, devs * slot_rows), 1)
    lane_slot = mod(lane, slot_rows)
    lane_id = ((div(lane, slot_rows) * pools + me_p) * slots + lane_slot).astype(F32)
    lane_id = jnp.where(lane_slot < slots, lane_id, -1.0)
    attn_picks = [
        jnp.where(column(line) == lane_id, 1.0, 0.0).astype(BF16) for line in own_rows
    ]
    gate_line = jnp.sum(
        jnp.where(ids_t[...] == me_d, gates_t[...], 0.0), axis=0, keepdims=True
    )
    route = column(gate_line)

    finish(sent)
    spread = dot(pick, g_query[...].reshape(cols, g_query.shape[2]))
    query = dot(jnp.where(own_g, spread[:, :half_w], 0.0).astype(BF16), fold)
    fresh = spread[:, half_w : half_w + pair]
    own_score = jnp.sum(query * fresh, axis=1, keepdims=True) * inv_root

    mixed = []
    position = iota((group, cache.shape[1]), 1).astype(F32)
    for s in range(slots):
        cache_copies[s].wait()
        at = slice(s * group, (s + 1) * group)
        entries = cache[s]
        scores = dot_nt(query[at].astype(BF16), entries) * inv_root
        scores = jnp.where(position < length[at], scores, -1e30)
        highest = jnp.maximum(jnp.max(scores, axis=1, keepdims=True), own_score[at])
        raised = jnp.exp(scores - highest)
        own_raised = jnp.exp(own_score[at] - highest)
        scale = 1.0 / (jnp.sum(raised, axis=1, keepdims=True) + own_raised)
        probs = (raised * scale).astype(BF16)
        own_prob = (own_raised * scale).astype(BF16).astype(F32)
        mixed.append(dot(probs, entries) + own_prob * fresh[at])
    mixed = jnp.concatenate(mixed, axis=0)
    values = mixed[:, head_dim:]
    twice = jnp.concatenate([values, values], axis=1)
    wide = jnp.concatenate([twice] * (group // 2), axis=1)
    own_block = div(iota((rows, width), 1), head_dim) == mod(iota((rows, width), 0), group)
    wide = jnp.where(own_block, wide, 0.0).astype(BF16)
    gather = jnp.where(
        div(iota((slot_rows, rows), 1), group) == iota((slot_rows, rows), 0), 1.0, 0.0
    ).astype(BF16)
    g_attn[me_d] = dot(gather, wide).astype(BF16)

    finish_attn = exchange("dev", me_d, devs, 1, g_attn)
    hidden_rows = hidden[...].astype(F32)
    partial = jnp.concatenate(
        [jnp.where(me_p == p, hidden_rows, 0.0) for p in range(pools)], axis=0
    )
    proj_copy.wait()
    finish(finish_attn)
    all_attn = g_attn[...].reshape(devs * slot_rows, width)
    for h in range(pool_heads):
        chosen = dot(attn_picks[h], all_attn).astype(BF16)
        partial = partial + dot_nt(chosen, proj_w[:, h * width : (h + 1) * width])

    pad = g_sum.shape[2] - col_block

    def padded(x):
        if not pad:
            return x
        return jnp.concatenate([x, jnp.zeros((x.shape[0], pad), x.dtype)], axis=1)

    g_sum[me_p] = padded(partial)
    finish(exchange("pool", me_p, pools, 0, g_sum))
    total = g_sum[0]
    for p in range(1, pools):
        total = total + g_sum[p]
    g_resid[me_d] = total.astype(BF16)

    finish(exchange("dev", me_d, devs, 2, g_resid))
    full = jnp.concatenate(
        [g_resid[d].astype(F32)[:, :col_block] for d in range(devs)], axis=1
    )
    mean = jnp.sum(full * full, axis=1, keepdims=True) * (1.0 / full.shape[1])
    normed = (full * lax.rsqrt(mean + 1e-05) * gain[...]).astype(BF16)

    acc[...] = jnp.zeros_like(acc)

    def expert(c, carry):
        in_copy(0, c).wait()
        in_copy(1, c).wait()
        gate = dot_nt(normed, in_w[0, c])
        up = dot_nt(normed, in_w[1, c])
        act = (gate * jax.nn.sigmoid(1.702 * gate) * (up + 1.0)).astype(BF16)
        down_copy(c).wait()
        acc[...] += dot(act, down_w[c])
        return carry

    lax.fori_loop(0, chunks, expert, 0)
    terms = acc[...] * route
    for d in range(devs):
        s_moe[d] = padded(terms[:, d * col_block : (d + 1) * col_block]).astype(BF16)
    g_moe[me_d] = s_moe[me_d]
    finish(exchange("dev", me_d, devs, 3, g_moe, s_moe))
    summed = g_moe[0].astype(F32)
    for d in range(1, devs):
        summed = summed + g_moe[d].astype(F32)
    g_last[me_p] = summed
    finish(exchange("pool", me_p, pools, 1, g_last))
    summed = g_last[0]
    for p in range(1, pools):
        summed = summed + g_last[p]
    result = summed + g_resid[me_d].astype(F32)
    mine = jnp.zeros((row_block, result.shape[1]), F32)
    for p in range(pools):
        mine = mine + jnp.where(me_p == p, result[p * row_block : (p + 1) * row_block], 0.0)
    out[...] = mine[:, :col_block].astype(BF16)


def body(
    devs,
    pools,
    hidden_in,
    queries,
    new_keyval,
    cache_entries,
    slot_table,
    context_len,
    out_proj,
    norm_gain,
    expert_ids,
    expert_gates,
    expert_in,
    expert_down,
):
    slots, context, pair = cache_entries.shape
    requests = slot_table.shape[0]
    pool_heads, width = queries.shape[1:]
    features = norm_gain.shape[0]
    hidden_units = expert_down.shape[1]
    col_block = hidden_in.shape[1]
    col_pad = up_to(col_block, 128)
    part = queries.shape[0] * pool_heads
    chunks = pieces(hidden_units)
    q = queries.reshape(part, width)
    kv = new_keyval.reshape(part, pair)
    pack = jnp.concatenate(
        [
            jnp.concatenate([q[:, : width // 2], kv], axis=1),
            jnp.concatenate([q[:, width // 2 :], kv], axis=1),
        ],
        axis=0,
    )
    slot_rows = up_to(slots, 16)
    depth = hidden_units // chunks
    vmem = pl.BlockSpec(memory_space=pltpu.VMEM)
    hbm = pl.BlockSpec(memory_space=pl.ANY)
    dma = pltpu.SemaphoreType.DMA
    return pl.pallas_call(
        functools.partial(kernel, devs, pools, pool_heads, slots, col_block),
        out_shape=jax.ShapeDtypeStruct(hidden_in.shape, BF16),
        in_specs=[vmem] * 7 + [hbm] * 4,
        out_specs=vmem,
        scratch_shapes=[
            pltpu.VMEM((slots, context, pair), BF16),
            pltpu.VMEM((out_proj.shape[1], out_proj.shape[0]), BF16),
            pltpu.VMEM((2, chunks, depth, features), BF16),
            pltpu.VMEM((chunks, depth, features), BF16),
            pltpu.VMEM((devs,) + pack.shape, BF16),
            pltpu.VMEM((devs, slot_rows, width), BF16),
            pltpu.VMEM((pools, requests, col_pad), F32),
            pltpu.VMEM((devs, requests, col_pad), BF16),
            pltpu.VMEM((devs, requests, col_pad), BF16),
            pltpu.VMEM((devs, requests, col_pad), BF16),
            pltpu.VMEM((pools, requests, col_pad), F32),
            pltpu.VMEM((requests, features), F32),
            dma((slots,)),
            dma((1,)),
            dma((2, chunks)),
            dma((chunks,)),
            dma((4, devs - 1)),
            dma((4, devs - 1)),
            dma((2, pools - 1)),
            dma((2, pools - 1)),
        ],
        compiler_params=pltpu.CompilerParams(
            collective_id=0, has_side_effects=True, vmem_limit_bytes=58 * 2**20
        ),
    )(
        hidden_in,
        pack,
        slot_table.T,
        context_len.reshape(1, requests),
        norm_gain.reshape(1, features),
        expert_ids.T,
        expert_gates.T,
        cache_entries,
        out_proj.T,
        expert_in[0].transpose(1, 2, 0).reshape(2, chunks, depth, features),
        expert_down.reshape(chunks, depth, features),
    )


def solution(mesh):
    return jax.shard_map(
        functools.partial(body, mesh.shape["dev"], mesh.shape["pool"]),
        mesh=mesh,
        in_specs=(
            P(("grp", "pool"), "dev"),
            P(("grp", "dev"), "pool", None),
            P(("grp", "dev"), "pool", None),
            P(("grp", "dev", "pool"), None, None),
            P("grp", None),
            P("grp"),
            P("pool", "dev"),
            P(),
            P("grp", None),
            P("grp", None),
            P("dev", None, None, "pool"),
            P("dev", "pool", None),
        ),
        out_specs=P(("grp", "pool"), "dev"),
        check_vma=False,
    )
```

time: 176 us -> 49 us (0.28)
  blocking collectives: 80.6 us -> 0 us
  waiting for transfers between devices: 52.2 us -> 0 us
  Pallas kernels: 0 us -> 43.9 us
  matrix products: 20.3 us -> 0 us
  between operations: 14.2 us -> 0.01 us
  other arithmetic: 3.28 us -> 1.36 us
    all_gather x4 -> x0, blocking collectives: 72.3 us -> none  [the longest x1 29.5 us: body(): blocks = lax.all_gather(residual[None], ('dev', 'pool'), axis=0, tiled=True)]
    unnamed x2 -> x0, waiting for transfers between devices: 52.2 us -> none
    pallas_call x0 -> x1, Pallas kernels: none -> 43.9 us  [body(): pl.pallas_call(functools.partial(kernel, devs, pools, pool_heads, slots,...]
    dot_general x9 -> x0, matrix products: 20.3 us -> none  [the longest x1 8.76 us: expert_apply(): jnp.dot(inputs, expert_in.reshape(expert_in.shape[1], 2 * hidden_units),...]
    unnamed x1 -> x0, blocking collectives: 8.31 us -> none
    reshape x3 -> x2, local copies, waits for them, and re-layouts: 0.17 us -> 2.02 us  [the longest x1 1.31 us: body(): norm_gain.reshape(1, features)]
  transfers between devices with their start and end apart: 1 -> 0, of which waited for: 1 -> 0; matrix products, arithmetic and copies ran while one was open for 0% -> 0% of each run, Pallas kernels for 0% -> 0%
where the time goes in v1:
time: 49 us; the launch traced here: 48.6 us
  Pallas kernels  43.9 us (90%)
  local copies, waits for them, and re-layouts  3.31 us (7%)
  other arithmetic  1.36 us (3%)
    pallas_call x1, Pallas kernels, body(): pl.pallas_call(functools.partial(kernel, devs, pools, pool_heads, slots,...  43.9 us
    concatenate x1, other arithmetic, body(): jnp.concatenate([jnp.concatenate([q[:, :width // 2], kv], axis=1), jnp.co...  1.36 us
    reshape x1, local copies, waits for them, and re-layouts, body(): norm_gain.reshape(1, features)  1.31 us
    unnamed x1, local copies, waits for them, and re-layouts  1.29 us

profile of v1, /device:TPU:0, one launch (start us, length us, event | category | flops | bytes accessed | tf_op | source)
XLA Modules:
  0.0 48.6 jit_solution(2631766179545410426)
XLA Ops:
  0.0 0.7 %reshape.18 = bf16[8,512]{1,0:T(8,128)(2,1)S(1)} reshape(bf16[2,4,512]{2,1,0:T(4,128)(2,1)} %param.13) | data formatting | bytes 16384 | tf_op jit(solution)/shard_map/reshape | solution.py:330
  0.7 1.4 %maximum_maximum_fusion.pack = bf16[16,384]{1,0:T(8,128)(2,1)} fusion(bf16[8,128]{1,0:T(8,128)(2,1)} %bitcast.18, bf16[8,256]{1,0:T(8,128)(2,1)S(1)} %get-tuple-element.6, bf16[8,256]{1,0:T(8,128)(2,1)S(1)} %get-tuple-element.5), kind=kLoop, calls=%fused_computation | loop fusion | flops 49152 | bytes 22528 | tf_op jit(solution)/shard_map/concatenate | solution.py:332
  2.1 1.3 %reshape.21.gain = f32[1,2880]{1,0:T(1,128)} reshape(f32[2880]{0:T(1024)} %param.19) | data formatting | bytes 23040 | tf_op jit(solution)/shard_map/reshape | solution.py:379
  3.4 43.9 %shard_map.118 = bf16[8,360]{1,0:T(8,128)(2,1)} custom-call(bf16[8,360]{1,0:T(8,128)(2,1)} %hidden.1, bf16[16,384]{1,0:T(8,128)(2,1)} %maximum_maximum_fusion.pack, s32[8,16]{1,0:T(8,128)} %bitcast.15, s32[1,16]{1,0:T(1,128)} %bitcast.19, f32[1,2880]{1,0:T(1,128)} %reshape.21.gain, s32[4,16]{1,0:T(4,128)} %bitcast.16, f32[4,16]{1,0:T(4,128)} %bitcast.17, ...), custom_call_target="tpu_custom_call" | custom-call | tf_op jit(solution)/shard_map/pallas_call | solution.py:344
  47.3 1.3 %copy.14 = bf16[8,360]{1,0:T(8,128)(2,1)} copy(bf16[8,360]{1,0:T(8,128)(2,1)} %shard_map.118) | data formatting | bytes 11520
  (1 shorter events, 0.0 us)

commit v2 on v1

--- a/solution.py
+++ b/solution.py
@@ -54,7 +54,8 @@
     slots,
     col_block,
     hidden,
-    pack,
+    queries,
+    new_keyval,
     table_t,
     lengths,
     gain,
@@ -95,7 +96,7 @@
     group = width // head_dim
     half_w = width // 2
     half_g = group // 2
-    pack_rows = pack.shape[0]
+    pack_rows = g_query.shape[1]
     part = pack_rows // 2
     per_dev = requests // devs
     chunks = in_w.shape[1]
@@ -155,7 +156,12 @@
         for copy in copies:
             copy.wait()
 
-    g_query[me_d] = pack[...]
+    count = queries.shape[0]
+    q = jnp.concatenate([queries[i].astype(F32) for i in range(count)], axis=0)
+    kv = jnp.concatenate([new_keyval[i].astype(F32) for i in range(count)], axis=0)
+    left = jnp.concatenate([q[:, :half_w], kv], axis=1)
+    right = jnp.concatenate([q[:, half_w:], kv], axis=1)
+    g_query[me_d] = jnp.concatenate([left, right], axis=0).astype(BF16)
     sent = exchange("dev", me_d, devs, 0, g_query)
 
     table = table_t[...].astype(F32)
@@ -267,7 +273,7 @@
         [g_resid[d].astype(F32)[:, :col_block] for d in range(devs)], axis=1
     )
     mean = jnp.sum(full * full, axis=1, keepdims=True) * (1.0 / full.shape[1])
-    normed = (full * lax.rsqrt(mean + 1e-05) * gain[...]).astype(BF16)
+    normed = (full * lax.rsqrt(mean + 1e-05) * gain[...].reshape(1, -1)).astype(BF16)
 
     acc[...] = jnp.zeros_like(acc)
 
@@ -327,15 +333,6 @@
     col_pad = up_to(col_block, 128)
     part = queries.shape[0] * pool_heads
     chunks = pieces(hidden_units)
-    q = queries.reshape(part, width)
-    kv = new_keyval.reshape(part, pair)
-    pack = jnp.concatenate(
-        [
-            jnp.concatenate([q[:, : width // 2], kv], axis=1),
-            jnp.concatenate([q[:, width // 2 :], kv], axis=1),
-        ],
-        axis=0,
-    )
     slot_rows = up_to(slots, 16)
     depth = hidden_units // chunks
     vmem = pl.BlockSpec(memory_space=pltpu.VMEM)
@@ -344,14 +341,14 @@
     return pl.pallas_call(
         functools.partial(kernel, devs, pools, pool_heads, slots, col_block),
         out_shape=jax.ShapeDtypeStruct(hidden_in.shape, BF16),
-        in_specs=[vmem] * 7 + [hbm] * 4,
+        in_specs=[vmem] * 8 + [hbm] * 4,
         out_specs=vmem,
         scratch_shapes=[
             pltpu.VMEM((slots, context, pair), BF16),
             pltpu.VMEM((out_proj.shape[1], out_proj.shape[0]), BF16),
             pltpu.VMEM((2, chunks, depth, features), BF16),
             pltpu.VMEM((chunks, depth, features), BF16),
-            pltpu.VMEM((devs,) + pack.shape, BF16),
+            pltpu.VMEM((devs, 2 * part, width // 2 + pair), BF16),
             pltpu.VMEM((devs, slot_rows, width), BF16),
             pltpu.VMEM((pools, requests, col_pad), F32),
             pltpu.VMEM((devs, requests, col_pad), BF16),
@@ -373,10 +370,11 @@
         ),
     )(
         hidden_in,
-        pack,
+        queries,
+        new_keyval,
         slot_table.T,
         context_len.reshape(1, requests),
-        norm_gain.reshape(1, features),
+        norm_gain,
         expert_ids.T,
         expert_gates.T,
         cache_entries,

time: 49 us -> 45.4 us (0.927)
  local copies, waits for them, and re-layouts: 3.31 us -> 1.29 us
  other arithmetic: 1.36 us -> 0 us
    reshape x2 -> x0, local copies, waits for them, and re-layouts: 2.02 us -> none  [the longest x1 1.31 us: body(): norm_gain.reshape(1, features)]
    concatenate x1 -> x0, other arithmetic: 1.36 us -> none  [body(): jnp.concatenate([jnp.concatenate([q[:, :width // 2], kv], axis=1), jnp.co...]
where the time goes in v2:
time: 45.4 us; the launch traced here: 45.2 us
  Pallas kernels  43.9 us (97%)
  local copies, waits for them, and re-layouts  1.29 us (3%)
    pallas_call x1, Pallas kernels, body(): pl.pallas_call(functools.partial(kernel, devs, pools, pool_heads, slots,...  43.9 us
    unnamed x1, local copies, waits for them, and re-layouts  1.29 us

profile of v2, /device:TPU:0, one launch (start us, length us, event | category | flops | bytes accessed | tf_op | source)
XLA Modules:
  0.0 45.2 jit_solution(11124432434577761737)
XLA Ops:
  0.0 43.9 %shard_map.118 = bf16[8,360]{1,0:T(8,128)(2,1)} custom-call(bf16[8,360]{1,0:T(8,128)(2,1)} %hidden.1, bf16[2,4,512]{2,1,0:T(4,128)(2,1)} %queries.1, bf16[2,4,128]{2,1,0:T(4,128)(2,1)} %new_keyval.1, s32[8,16]{1,0:T(8,128)} %bitcast.14, s32[1,16]{1,0:T(1,128)} %bitcast.17, f32[2880]{0:T(1024)} %gain.1, s32[4,16]{1,0:T(4,128)} %bitcast.15, f32[4,16]{1,0:T(4,128)} %bitcast.16, ...), custom_call_target="tpu_custom_call" | custom-call | tf_op jit(solution)/shard_map/pallas_call | solution.py:341
  43.9 1.3 %copy.14 = bf16[8,360]{1,0:T(8,128)(2,1)} copy(bf16[8,360]{1,0:T(8,128)(2,1)} %shard_map.118) | data formatting | bytes 11520

commit v3 on v2

--- a/solution.py
+++ b/solution.py
@@ -76,7 +76,6 @@
     g_resid,
     s_moe,
     g_moe,
-    g_last,
     acc,
     cache_sem,
     proj_sem,
@@ -86,6 +85,8 @@
     dev_recv,
     pool_send,
     pool_recv,
+    all_send,
+    all_recv,
 ):
     me_d, me_p = lax.axis_index("dev"), lax.axis_index("pool")
     requests = table_t.shape[1]
@@ -118,30 +119,29 @@
     def down_copy(c):
         return pltpu.make_async_copy(down_hbm.at[c], down_w.at[c], down_sem.at[c])
 
-    for c in range(chunks):
-        in_copy(0, c).start()
-        in_copy(1, c).start()
-        down_copy(c).start()
-
     barrier = pltpu.get_barrier_semaphore()
-    for axis, me, n in (("dev", me_d, devs), ("pool", me_p, pools)):
-        for k in range(1, n):
-            pl.semaphore_signal(
-                barrier,
-                inc=1,
-                device_id={axis: lax.rem(me + k, n)},
-                device_id_type=pl.DeviceIdType.MESH,
-            )
-    pl.semaphore_wait(barrier, devs + pools - 2)
-
-    def exchange(axis, me, n, phase, dst, source=None):
+    steps = [(i, j) for i in range(devs) for j in range(pools)][1:]
+
+    def partner(step):
+        return {"dev": lax.rem(me_d + step[0], devs), "pool": lax.rem(me_p + step[1], pools)}
+
+    for step in steps:
+        pl.semaphore_signal(
+            barrier,
+            inc=1,
+            device_id=partner(step),
+            device_id_type=pl.DeviceIdType.MESH,
+        )
+    pl.semaphore_wait(barrier, len(steps))
+
+    def exchange(axis, me, n, phase, dst):
         send, recv = (dev_send, dev_recv) if axis == "dev" else (pool_send, pool_recv)
         copies = []
         for k in range(1, n):
             peer = lax.rem(me + k, n)
             copies.append(
                 pltpu.make_async_remote_copy(
-                    src_ref=dst.at[me] if source is None else source.at[peer],
+                    src_ref=dst.at[me],
                     dst_ref=dst.at[me],
                     send_sem=send.at[phase, k - 1],
                     recv_sem=recv.at[phase, k - 1],
@@ -211,6 +211,11 @@
     route = column(gate_line)
 
     finish(sent)
+    for c in range(chunks):
+        in_copy(0, c).start()
+        in_copy(1, c).start()
+        down_copy(c).start()
+
     spread = dot(pick, g_query[...].reshape(cols, g_query.shape[2]))
     query = dot(jnp.where(own_g, spread[:, :half_w], 0.0).astype(BF16), fold)
     fresh = spread[:, half_w : half_w + pair]
@@ -287,25 +292,50 @@
         acc[...] += dot(act, down_w[c])
         return carry
 
-    lax.fori_loop(0, chunks, expert, 0)
+    for c in range(chunks):
+        expert(c, 0)
     terms = acc[...] * route
+    split = s_moe.shape[3]
+    wide_block = g_sum.shape[2]
     for d in range(devs):
-        s_moe[d] = padded(terms[:, d * col_block : (d + 1) * col_block]).astype(BF16)
-    g_moe[me_d] = s_moe[me_d]
-    finish(exchange("dev", me_d, devs, 3, g_moe, s_moe))
-    summed = g_moe[0].astype(F32)
-    for d in range(1, devs):
-        summed = summed + g_moe[d].astype(F32)
-    g_last[me_p] = summed
-    finish(exchange("pool", me_p, pools, 1, g_last))
-    summed = g_last[0]
-    for p in range(1, pools):
-        summed = summed + g_last[p]
-    result = summed + g_resid[me_d].astype(F32)
-    mine = jnp.zeros((row_block, result.shape[1]), F32)
+        block = padded(terms[:, d * col_block : (d + 1) * col_block])
+        for p in range(pools):
+            piece = block[p * row_block : (p + 1) * row_block]
+            if split < wide_block:
+                rest = piece[:, split:]
+                fill = jnp.zeros((row_block, 2 * split - wide_block), F32)
+                if fill.shape[1]:
+                    rest = jnp.concatenate([rest, fill], axis=1)
+                piece = jnp.concatenate([piece[:, :split], rest], axis=0)
+            s_moe[d, p] = piece.astype(BF16)
+    g_moe[me_d, me_p] = s_moe[me_d, me_p]
+    copies = []
+    for k, step in enumerate(steps):
+        target = partner(step)
+        copies.append(
+            pltpu.make_async_remote_copy(
+                src_ref=s_moe.at[target["dev"], target["pool"]],
+                dst_ref=g_moe.at[me_d, me_p],
+                send_sem=all_send.at[k],
+                recv_sem=all_recv.at[k],
+                device_id=target,
+                device_id_type=pl.DeviceIdType.MESH,
+            )
+        )
+        copies[-1].start()
+    resid = g_resid[me_d].astype(F32)
+    mine = jnp.zeros((row_block, wide_block), F32)
     for p in range(pools):
-        mine = mine + jnp.where(me_p == p, result[p * row_block : (p + 1) * row_block], 0.0)
-    out[...] = mine[:, :col_block].astype(BF16)
+        mine = mine + jnp.where(me_p == p, resid[p * row_block : (p + 1) * row_block], 0.0)
+    finish(copies)
+    summed = jnp.sum(
+        g_moe[...].reshape((devs * pools,) + s_moe.shape[2:]).astype(F32), axis=0
+    )
+    if split < wide_block:
+        summed = jnp.concatenate(
+            [summed[:row_block], summed[row_block:, : wide_block - split]], axis=1
+        )
+    out[...] = (mine + summed)[:, :col_block].astype(BF16)
 
 
 def body(
@@ -333,6 +363,10 @@
     col_pad = up_to(col_block, 128)
     part = queries.shape[0] * pool_heads
     chunks = pieces(hidden_units)
+    row_block = hidden_in.shape[0]
+    moe_block = (row_block, col_pad)
+    if row_block % 16:
+        moe_block = (2 * row_block, up_to(-(-col_pad // 2), 128))
     slot_rows = up_to(slots, 16)
     depth = hidden_units // chunks
     vmem = pl.BlockSpec(memory_space=pltpu.VMEM)
@@ -352,18 +386,19 @@
             pltpu.VMEM((devs, slot_rows, width), BF16),
             pltpu.VMEM((pools, requests, col_pad), F32),
             pltpu.VMEM((devs, requests, col_pad), BF16),
-            pltpu.VMEM((devs, requests, col_pad), BF16),
-            pltpu.VMEM((devs, requests, col_pad), BF16),
-            pltpu.VMEM((pools, requests, col_pad), F32),
+            pltpu.VMEM((devs, pools) + moe_block, BF16),
+            pltpu.VMEM((devs, pools) + moe_block, BF16),
             pltpu.VMEM((requests, features), F32),
             dma((slots,)),
             dma((1,)),
             dma((2, chunks)),
             dma((chunks,)),
-            dma((4, devs - 1)),
-            dma((4, devs - 1)),
-            dma((2, pools - 1)),
-            dma((2, pools - 1)),
+            dma((3, devs - 1)),
+            dma((3, devs - 1)),
+            dma((1, pools - 1)),
+            dma((1, pools - 1)),
+            dma((devs * pools - 1,)),
+            dma((devs * pools - 1,)),
         ],
         compiler_params=pltpu.CompilerParams(
             collective_id=0, has_side_effects=True, vmem_limit_bytes=58 * 2**20

time: 45.4 us -> 44.3 us (0.976)
  Pallas kernels: 43.9 us -> 42.7 us
    pallas_call x1, Pallas kernels: 43.9 us -> 42.7 us  [body(): pl.pallas_call(functools.partial(kernel, devs, pools, pool_heads, slots,...]
where the time goes in v3:
time: 44.3 us; the launch traced here: 44 us
  Pallas kernels  42.7 us (96%)
  local copies, waits for them, and re-layouts  1.29 us (3%)
    pallas_call x1, Pallas kernels, body(): pl.pallas_call(functools.partial(kernel, devs, pools, pool_heads, slots,...  42.7 us
    unnamed x1, local copies, waits for them, and re-layouts  1.29 us

profile of v3, /device:TPU:0, one launch (start us, length us, event | category | flops | bytes accessed | tf_op | source)
XLA Modules:
  0.0 44.0 jit_solution(4252276204587581614)
XLA Ops:
  0.0 42.7 %shard_map.118 = bf16[8,360]{1,0:T(8,128)(2,1)} custom-call(bf16[8,360]{1,0:T(8,128)(2,1)} %hidden.1, bf16[2,4,512]{2,1,0:T(4,128)(2,1)} %queries.1, bf16[2,4,128]{2,1,0:T(4,128)(2,1)} %new_keyval.1, s32[8,16]{1,0:T(8,128)} %bitcast.14, s32[1,16]{1,0:T(1,128)} %bitcast.17, f32[2880]{0:T(1024)} %gain.1, s32[4,16]{1,0:T(4,128)} %bitcast.15, f32[4,16]{1,0:T(4,128)} %bitcast.16, ...), custom_call_target="tpu_custom_call" | custom-call | tf_op jit(solution)/shard_map/pallas_call | solution.py:375
  42.7 1.3 %copy.14 = bf16[8,360]{1,0:T(8,128)(2,1)} copy(bf16[8,360]{1,0:T(8,128)(2,1)} %shard_map.118) | data formatting | bytes 11520

commit v4 on v3

--- a/solution.py
+++ b/solution.py
@@ -33,7 +33,7 @@
 
 
 def pieces(rows):
-    for count in (6, 5, 4, 3, 2):
+    for count in (3, 2):
         if rows % count == 0 and (rows // count) % 16 == 0:
             return count
     return 1

time: 44.3 us -> 43.3 us (0.977)
  Pallas kernels: 42.7 us -> 41.8 us
    pallas_call x1, Pallas kernels: 42.7 us -> 41.8 us  [body(): pl.pallas_call(functools.partial(kernel, devs, pools, pool_heads, slots,...]
where the time goes in v4:
time: 43.3 us; the launch traced here: 43.1 us
  Pallas kernels  41.8 us (97%)
  local copies, waits for them, and re-layouts  1.29 us (3%)
    pallas_call x1, Pallas kernels, body(): pl.pallas_call(functools.partial(kernel, devs, pools, pool_heads, slots,...  41.8 us
    unnamed x1, local copies, waits for them, and re-layouts  1.29 us

profile of v4, /device:TPU:0, one launch (start us, length us, event | category | flops | bytes accessed | tf_op | source)
XLA Modules:
  0.0 43.1 jit_solution(9062425617990406823)
XLA Ops:
  0.0 41.8 %shard_map.118 = bf16[8,360]{1,0:T(8,128)(2,1)} custom-call(bf16[8,360]{1,0:T(8,128)(2,1)} %hidden.1, bf16[2,4,512]{2,1,0:T(4,128)(2,1)} %queries.1, bf16[2,4,128]{2,1,0:T(4,128)(2,1)} %new_keyval.1, s32[8,16]{1,0:T(8,128)} %bitcast.14, s32[1,16]{1,0:T(1,128)} %bitcast.17, f32[2880]{0:T(1024)} %gain.1, s32[4,16]{1,0:T(4,128)} %bitcast.15, f32[4,16]{1,0:T(4,128)} %bitcast.16, ...), custom_call_target="tpu_custom_call" | custom-call | tf_op jit(solution)/shard_map/pallas_call | solution.py:375
  41.8 1.3 %copy.14 = bf16[8,360]{1,0:T(8,128)(2,1)} copy(bf16[8,360]{1,0:T(8,128)(2,1)} %shard_map.118) | data formatting | bytes 11520
